TPU v7x, 256 devices: a whole 4x4x8 slice. The times are simulated.
256 devices in a mesh: ep: 16 (over x_lo, z), fsdp: 8 (over y, x_hi), rep: 2 (over core).
Axes of the slice: x: 4 (x_hi: 2, x_lo: 2; x = x_hi * 2 + x_lo), y: 4, z: 8, core: 2. Of those that a mesh axis runs over, the one named last changes fastest.
Arguments:
- weights: bfloat16 [32, 2048, 7168], P(('ep', 'rep'), None, 'fsdp'), may hold values from -6 to 6
- owner_map: int32 [32], replicated, may hold values from 0 to 63
Outputs:
- quant: bfloat16 [32, 8, 256, 7168], P(None, 'fsdp', ('ep', 'rep'))
- block_scales: float32 [32, 16, 56], P(None, 'fsdp')
All inputs are finite; a program needn't handle non-finite values. Where the computation divides by a largest or mean magnitude, that divisor is 1e-20 or more.
Results may differ from a plain program's by a relative error of at most 0.0057.
Values may be sent and summed in bfloat16 or wider, within the bound.
A program may use at most 64 MiB of HBM per device.

v0:
```python
import math

import jax
import jax.numpy as jnp
from jax import lax
from jax.sharding import PartitionSpec as P

D = 7168
HAD = 128
QB = 128
COS = 56


epsilon = 1e-06


def tables():
    lane_ids = jnp.arange(HAD, dtype=jnp.int32)
    anded = jnp.bitwise_and(lane_ids[:, None], lane_ids[None, :])
    parity = jnp.zeros((HAD, HAD), jnp.int32)
    for bit_pos in range(HAD.bit_length() - 1):
        parity = parity + jnp.bitwise_and(jnp.right_shift(anded, bit_pos), 1)
    signs_table = (1 - 2 * (parity % 2)).astype(jnp.float32).astype(jnp.bfloat16)
    freq_ids = jnp.arange(COS, dtype=jnp.float32)[:, None]
    cell_ids = jnp.arange(COS, dtype=jnp.float32)[None, :]
    cosine = jnp.sqrt(jnp.float32(2.0 / COS)) * jnp.cos(
        jnp.float32(math.pi) * (2.0 * cell_ids + 1.0) * freq_ids / (2.0 * COS)
    )
    cosine = jnp.where(freq_ids == 0.0, cosine * jnp.float32(math.sqrt(0.5)), cosine)
    return (signs_table, cosine.astype(jnp.bfloat16))


def positions(owner_map):
    count = owner_map.shape[0]
    expert_ids = jnp.arange(count, dtype=jnp.int32)
    before = (owner_map[None, :] < owner_map[:, None]) | (
        owner_map[None, :] == owner_map[:, None]
    ) & (expert_ids[None, :] < expert_ids[:, None])
    place = jnp.sum(before.astype(jnp.int32), axis=1)
    chosen = jnp.where(place[None, :] == expert_ids[:, None], expert_ids[None, :], 0)
    return jnp.sum(chosen, axis=1)


def per_device(weights, owner_map):
    experts_here, row_count, width_here = weights.shape
    signs_table, cos_table = tables()
    pieces = lax.axis_size("fsdp")
    inv_root = jnp.float32(1.0 / math.sqrt(HAD))
    split_parts = weights.reshape(experts_here, row_count, width_here // HAD, HAD)
    half_flat = (
        jnp.einsum("erji,ih->erjh", split_parts, signs_table, preferred_element_type=jnp.float32)
        * inv_root
    ).astype(jnp.bfloat16)
    blocks_each = row_count // pieces // QB
    total = owner_map.shape[0]
    new_order = positions(owner_map)
    half_turned = half_flat.reshape(experts_here, pieces, blocks_each, QB, width_here)
    turned = lax.all_to_all(half_turned, "fsdp", split_axis=1, concat_axis=4, tiled=True)
    block_count = turned.shape[2]
    grouped = turned.reshape(experts_here, block_count, QB, COS, HAD)
    rotated = jnp.einsum("kj,ebrjh->ebrkh", cos_table, grouped, preferred_element_type=jnp.float32)
    block_scale = jnp.max(jnp.abs(rotated), axis=(2, 4)) + jnp.float32(epsilon)
    scaled = (rotated / block_scale[:, :, None, :, None]).astype(jnp.bfloat16)
    scaled, block_scale = (
        scaled.reshape(experts_here, 1, block_count, QB, D),
        block_scale.reshape(experts_here, 1, block_count, COS),
    )
    scaled = scaled.reshape(experts_here, row_count // pieces, D)
    block_scale = block_scale.reshape(experts_here, blocks_each, COS)
    arrived = lax.all_to_all(scaled, ("ep", "rep"), split_axis=1, concat_axis=0, tiled=True)
    all_scales = lax.all_gather(block_scale, ("ep", "rep"), axis=0, tiled=True)
    quant = jnp.take(arrived, new_order, axis=0).reshape(total, 1, arrived.shape[1], D)
    block_scales = jnp.take(all_scales, new_order, axis=0)
    return (quant, block_scales)


def solution(mesh):
    placed = (P(("ep", "rep"), None, "fsdp"), P())
    return jax.shard_map(
        per_device,
        mesh=mesh,
        in_specs=placed,
        out_specs=(P(None, "fsdp", ("ep", "rep"), None), P(None, "fsdp", None)),
        check_vma=False,
    )
```

profile of v0, /device:TPU:8, one launch (start us, length us, event | category | flops | bytes accessed | tf_op | source)
XLA Modules:
  0.0 295.3 jit_solution(5329059766649407702)
XLA Ops:
  0.6 6.1 %copy.20 = bf16[1,2048,896]{1,2,0:T(8,128)(2,1)} copy(bf16[1,2048,896]{2,1,0:T(8,128)(2,1)} %param.2) | data formatting | bytes 7340032 | tf_op args[0]
  6.7 5.0 %fusion.4 = bf16[2048,7,128]{0,2,1:T(8,128)(2,1)} fusion(bf16[2048,7,128]{0,2,1:T(8,128)(2,1)} %bitcast.54), kind=kOutput, calls=%fused_computation.11 | convolution fusion | flops 474021888 | bytes 7340032 | tf_op jit(solution)/shard_map/erji,ih->erjh/dot_general | solution.py:51
  11.7 7.1 %reshape.87 = bf16[1,8,2,128,896]{3,2,1,4,0:T(2,128)(2,1)} reshape(bf16[2048,7,128]{0,2,1:T(8,128)(2,1)} %fusion.4) | data formatting | bytes 7340032 | tf_op jit(solution)/shard_map/reshape | solution.py:57
  18.7 6.4 %copy.22 = bf16[1,8,2,128,896]{3,2,4,0,1:T(2,128)(2,1)} copy(bf16[1,8,2,128,896]{3,2,1,4,0:T(2,128)(2,1)} %reshape.87) | data formatting | bytes 7340032 | tf_op jit(solution)/shard_map/reshape | solution.py:57
  25.1 7.4 %all-to-all-start = ((bf16[1,8,2,128,896]{3,2,4,0,1:T(2,128)(2,1)}), bf16[1,8,2,128,896]{3,2,4,0,1:T(2,128)(2,1)}, u32[]{:S(2)}, u32[]{:S(2)}) async-start(bf16[1,8,2,128,896]{3,2,4,0,1:T(2,128)(2,1)} %copy.22), calls=%async_computation | async-start | bytes 7340032 | tf_op jit(solution)/shard_map/all_to_all | solution.py:58
  32.5 43.6 %all-to-all-done = bf16[1,8,2,128,896]{3,2,4,0,1:T(2,128)(2,1)} async-done(((bf16[1,8,2,128,896]{3,2,4,0,1:T(2,128)(2,1)}), bf16[1,8,2,128,896]{3,2,4,0,1:T(2,128)(2,1)}, u32[]{:S(2)}, u32[]{:S(2)}) %all-to-all-start) | async-done | bytes 3670048 | tf_op jit(solution)/shard_map/all_to_all | solution.py:58
  76.2 7.2 %copy.28 = bf16[2,128,56,128]{3,2,1,0:T(8,128)(2,1)} copy(bf16[2,128,56,128]{1,0,3,2:T(2,128)(2,1)} %bitcast.5) | data formatting | bytes 7340032 | tf_op jit(solution)/shard_map/reshape.8
  83.4 3.3 %fusion = (f32[2,56]{1,0:T(2,128)S(1)}, f32[2,128,128,56]{2,3,1,0:T(8,128)S(1)}) fusion(bf16[2,128,56,128]{3,2,1,0:T(8,128)(2,1)} %copy.28, f32[56]{0:T(128)S(1)} %add_multiply_fusion, pred[56]{0:T(512)(128)(4,1)S(1)} %iota_compare_fusion.2), kind=kOutput, calls=%fused_computation.4 | convolution fusion | flops 209209616 | bytes 11010776 | tf_op jit(solution)/shard_map/kj,ebrjh->ebrkh/dot_general | solution.py:61
  86.7 2.5 fusion.3
  89.2 19.7 %reshape_reshape.4 = bf16[1,256,7168]{2,0,1:T(2,128)(2,1)} reshape(bf16[1,2,128,56,128]{4,3,2,1,0:T(8,128)(2,1)} %fusion.3) | data formatting | bytes 7340032 | tf_op jit(solution)/shard_map/reshape;reshape | solution.py:68
  108.9 0.5 broadcast.108
  109.5 23.1 %reduce.2 = bf16[256,7168]{1,0:T(8,128)(2,1)} reduce(bf16[256,1,7168]{2,1,0:T(2,128)(2,1)} %bitcast.52, bf16[]{:T(256)} %broadcast.108), dimensions={1}, to_apply=%bitcast.45.reduce_sub_computation | reduce | bytes 7340034
  132.5 8.9 %reshape.111 = bf16[32,2,28672]{2,1,0:T(2,128)(2,1)} reshape(bf16[256,7168]{1,0:T(8,128)(2,1)} %reduce.2) | data formatting | bytes 7340032
  141.4 0.0 copy-start
  141.4 9.1 %all-to-all-start.1 = ((bf16[32,2,28672]{2,1,0:T(2,128)(2,1)}), bf16[32,2,28672]{2,1,0:T(2,128)(2,1)}, u32[]{:S(2)}, u32[]{:S(2)}) async-start(bf16[32,2,28672]{2,1,0:T(2,128)(2,1)} %reshape.111), calls=%async_computation.1 | async-start | bytes 7340032 | tf_op jit(solution)/shard_map/all_to_all | solution.py:70
  150.5 0.0 copy-done
  150.5 0.2 convert_reduce_fusion
  150.7 0.1 select_reduce_fusion
  150.9 108.8 %all-gather.1 = f32[32,2,56]{2,1,0:T(2,128)S(1)} all-gather(f32[1,2,56]{2,1,0:T(2,128)S(1)} %get-tuple-element.6), channel_id=2, replica_groups=mesh['ep'=16,'fsdp'=8,'rep'=2] {'ep','rep'}, dimensions={0}, use_global_device_ids=true | all-gather | bytes 14784 | tf_op jit(solution)/shard_map/all_gather | solution.py:71
  259.7 0.6 gather_fusion.1
  260.3 0.7 broadcast_select_fusion
  261.0 0.0 all-to-all-done.1
  261.0 19.3 %reshape.112 = bf16[256,1,7168]{2,1,0:T(2,128)(2,1)} reshape(bf16[32,2,28672]{2,1,0:T(2,128)(2,1)} %all-to-all-done.1) | data formatting | bytes 7340032
  280.4 6.0 %copy.31 = bf16[1,256,7168]{2,1,0:T(8,128)(2,1)} copy(bf16[1,256,7168]{2,0,1:T(2,128)(2,1)} %bitcast.53) | data formatting | bytes 7340032
  286.4 4.6 %gather_fusion = bf16[32,8,7168]{2,1,0:T(8,128)(2,1)} fusion(bf16[32,8,7168]{2,1,0:T(8,128)(2,1)} %bitcast.55, s32[1024]{0:T(1024)S(1)} %pad_clamp_fusion), kind=kCustom, calls=%fused_computation | custom fusion | bytes 7340160 | tf_op jit(solution)/shard_map/jit(_take)/gather | solution.py:72
  291.0 4.3 %fusion.2 = bf16[32,1,8,7168]{3,2,1,0:T(8,128)(2,1)} fusion(bf16[32,8,7168]{2,1,0:T(8,128)(2,1)} %gather_fusion, pred[32]{0:T(512)(128)(4,1)S(1)} %compare_and_fusion), kind=kLoop, calls=%fused_computation.9 | loop fusion | flops 1835008 | bytes 7340064
  (6 shorter events, 0.0 us)
Async XLA Ops:
  25.1 51.0 %all-to-all-start = ((bf16[1,8,2,128,896]{3,2,4,0,1:T(2,128)(2,1)}), bf16[1,8,2,128,896]{3,2,4,0,1:T(2,128)(2,1)}, u32[]{:S(2)}, u32[]{:S(2)}) async-start(bf16[1,8,2,128,896]{3,2,4,0,1:T(2,128)(2,1)} %copy.22), calls=%async_computation | async-start | bytes 7340032 | tf_op jit(solution)/shard_map/all_to_all | solution.py:58
  141.4 9.1 %copy-start = (s32[32]{0:T(128)S(1)}, s32[32]{0:T(128)}, u32[]{:S(2)}) copy-start(s32[32]{0:T(128)} %param.3) | copy-start | bytes 388
  141.4 119.7 %all-to-all-start.1 = ((bf16[32,2,28672]{2,1,0:T(2,128)(2,1)}), bf16[32,2,28672]{2,1,0:T(2,128)(2,1)}, u32[]{:S(2)}, u32[]{:S(2)}) async-start(bf16[32,2,28672]{2,1,0:T(2,128)(2,1)} %reshape.111), calls=%async_computation.1 | async-start | bytes 7340032 | tf_op jit(solution)/shard_map/all_to_all | solution.py:70
where the time goes:
time: 300 us; the launch traced here: 295 us
  blocking collectives  109 us (36%)
  local copies, waits for them, and re-layouts  86.4 us (29%)
  waiting for transfers between devices  43.6 us (15%)
  other arithmetic  30.9 us (10%)
  starting transfers between devices  16.5 us (6%)
  matrix products  8.3 us (3%)
    all_gather x1, blocking collectives, per_device(): all_scales = lax.all_gather(block_scale, ('ep', 'rep'), axis=0, tiled=True)  109 us
    all_to_all x1, waiting for transfers between devices, per_device(): lax.all_to_all(half_turned, 'fsdp', split_axis=1, concat_axis=4, tiled=True)  43.6 us
    unnamed x7, local copies, waits for them, and re-layouts  40.8 us
    unnamed x3, other arithmetic  27.4 us
    another operation x1, local copies, waits for them, and re-layouts, per_device(): scaled = scaled.reshape(experts_here, row_count // pieces, D)  19.7 us
    reshape x2, local copies, waits for them, and re-layouts, per_device(): half_flat.reshape(experts_here, pieces, blocks_each, QB, width_here)  13.4 us
    all_to_all x1, starting transfers between devices, per_device(): lax.all_to_all(scaled, ('ep', 'rep'), split_axis=1, concat_axis=0, tiled=...  9.13 us
    all_to_all x1, starting transfers between devices, per_device(): lax.all_to_all(half_turned, 'fsdp', split_axis=1, concat_axis=4, tiled=True)  7.38 us
  transfers between devices with their start and end apart: 2, of which 1 were waited for; matrix products, arithmetic and copies ran while one was open for 1% of the time, Pallas kernels for 0%

commit v1 on v0

v1 whole, which is shorter than its diff:
```python
import math

import jax
import jax.numpy as jnp
import ml_dtypes
import numpy as np
from jax import lax
from jax.experimental import pallas as pl
from jax.experimental.pallas import tpu as pltpu
from jax.sharding import PartitionSpec as P

MESH = pl.DeviceIdType.MESH
D = 7168
HAD = 128
COS = 56
WIDE = 896
TILES = WIDE // HAD
ROWS = 16
WAVES = 8
GROUP = 16
EPS = 1e-06


def hadamard():
    i = np.arange(HAD)
    both = i[:, None] & i[None, :]
    ones = sum((both >> bit) & 1 for bit in range(7))
    return (1 - 2 * (ones % 2)).astype(np.float32)


def cosine():
    k = np.arange(COS, dtype=np.float64)[:, None]
    j = np.arange(COS, dtype=np.float64)[None, :]
    c = np.sqrt(2.0 / COS) * np.cos(np.pi * (2 * j + 1) * k / (2 * COS))
    c[0] *= np.sqrt(0.5)
    return c.astype(ml_dtypes.bfloat16).astype(np.float32)


def positions(owner_map):
    count = owner_map.shape[0]
    ids = jnp.arange(count, dtype=jnp.int32)
    before = (owner_map[None, :] < owner_map[:, None]) | (
        (owner_map[None, :] == owner_map[:, None]) & (ids[None, :] < ids[:, None])
    )
    place = jnp.sum(before.astype(jnp.int32), axis=1)
    chosen = jnp.where(place[None, :] == ids[:, None], ids[None, :], 0)
    return jnp.sum(chosen, axis=1)


def device(z, x, y, c):
    return (lax.rem(x, 2) * 8 + z, y * 2 + x // 2, c)


def place():
    ep, fsdp, core = lax.axis_index("ep"), lax.axis_index("fsdp"), lax.axis_index("rep")
    return lax.rem(ep, 8), lax.rem(fsdp, 2) * 2 + ep // 8, fsdp // 2, core


def wave_step(i):
    return 4 + (1 - 2 * lax.rem(i, 2)) * ((i + 1) // 2)


def move_kernel(
    w_ref, had_ref, mix_ref, out_ref, scales_ref,
    w_buf, half, turned, res, sent, top, mine,
    w_sem, b_send, b_recv, a_send, a_recv, keep_sem, pair_sem, s_send, s_recv,
):
    z, x, y, c = place()
    here = y * 4 + x
    slot = z * 2 + c
    low = lax.rem(x, 2)

    barrier = pltpu.get_barrier_semaphore()
    for dz in range(8):
        for dc in range(2):
            if dz or dc:
                pl.semaphore_signal(
                    barrier, inc=1, device_id_type=MESH,
                    device_id=device(lax.rem(z + dz, 8), x, y, lax.rem(c + dc, 2)),
                )
    for o in range(1, GROUP):
        pl.semaphore_signal(
            barrier, inc=1, device_id_type=MESH,
            device_id=device(z, lax.rem(x + o % 4, 4), lax.rem(y + o // 4, 4), c),
        )

    def goes_to(i):
        return lax.rem(z + wave_step(i), 8)

    def fetch(i):
        return pltpu.make_async_copy(w_ref.at[:, goes_to(i)], w_buf.at[i], w_sem.at[i])

    @pl.loop(0, WAVES)
    def _(i):
        fetch(i).start()

    top[...] = jnp.zeros_like(top)

    def turn(i):
        fetch(i).wait()
        rows = w_buf[i].reshape(GROUP * ROWS, WIDE)
        for first in range(0, WIDE, 256):
            wide = min(256, WIDE - first)
            got = jnp.dot(
                rows[:, first : first + wide], had_ref[:wide, :wide], preferred_element_type=jnp.float32
            ) * jnp.float32(1.0 / math.sqrt(HAD))
            half[i, :, :, first : first + wide] = got.astype(jnp.bfloat16).reshape(GROUP, ROWS, wide)
        turned[i, here] = half[i, here]

    def spread(i):
        @pl.loop(1, GROUP)
        def _(o):
            to_x, to_y = lax.rem(x + lax.rem(o, 4), 4), lax.rem(y + o // 4, 4)
            pltpu.make_async_remote_copy(
                src_ref=half.at[i, to_y * 4 + to_x],
                dst_ref=turned.at[i, here],
                send_sem=b_send,
                recv_sem=b_recv.at[i],
                device_id=device(z, to_x, to_y, c),
                device_id_type=MESH,
            ).start()

    turn(0)
    pl.semaphore_wait(barrier, 30)
    spread(0)

    @pl.loop(0, WAVES)
    def _(i):
        @pl.when(i < WAVES - 1)
        def _():
            turn(i + 1)
            spread(i + 1)

        landed = turned.at[i, pl.ds(0, GROUP - 1)]
        pltpu.make_async_copy(landed, landed, b_recv.at[i]).wait()

        cells = [
            jnp.concatenate(
                [
                    turned[i, f * 2 + e, :, t * HAD : (t + 1) * HAD]
                    for f in range(8)
                    for t in range(TILES)
                ],
                axis=0,
            )
            for e in range(2)
        ]
        res[...] = jnp.dot(
            mix_ref[...], jnp.concatenate(cells, axis=1), preferred_element_type=jnp.float32
        )
        for k in range(COS):
            for e in range(2):
                best = top[e, k]
                for to_c in range(2):
                    got = res[k * ROWS + to_c * 8 : k * ROWS + to_c * 8 + 8, e * HAD : (e + 1) * HAD]
                    best = jnp.maximum(best, jnp.abs(got))
                    sent[i, to_c, e, :, k * HAD : (k + 1) * HAD] = got.astype(jnp.bfloat16)
                top[e, k] = best

        to_z = goes_to(i)

        def ship(to_c):
            pltpu.make_async_remote_copy(
                src_ref=sent.at[i, to_c],
                dst_ref=out_ref.at[slot],
                send_sem=a_send,
                recv_sem=a_recv,
                device_id=device(to_z, x, y, to_c),
                device_id_type=MESH,
            ).start()

        ship(1 - c)

        @pl.when(i < WAVES - 1)
        def _():
            ship(c)

    keep = pltpu.make_async_copy(sent.at[WAVES - 1, c], out_ref.at[slot], keep_sem)
    keep.start()

    largest = jnp.max(jnp.max(top[...], axis=2), axis=2, keepdims=True) + jnp.float32(EPS)
    diagonal = lax.broadcasted_iota(jnp.int32, (COS, HAD), 0) == lax.broadcasted_iota(
        jnp.int32, (COS, HAD), 1
    )
    lines = [
        jnp.sum(jnp.where(diagonal, largest[e], 0.0), axis=0, keepdims=True) for e in range(2)
    ]
    mine[low] = jnp.concatenate(lines + [jnp.zeros((6, HAD), jnp.float32)], axis=0)

    pair = pltpu.make_async_remote_copy(
        src_ref=mine.at[low],
        dst_ref=mine.at[low],
        send_sem=pair_sem.at[0],
        recv_sem=pair_sem.at[1],
        device_id=device(z, x + 1 - 2 * low, y, c),
        device_id_type=MESH,
    )
    pair.start()
    pair.wait()
    scales_ref[slot] = mine[...]

    @pl.loop(1, GROUP)
    def _(o):
        pltpu.make_async_remote_copy(
            src_ref=mine,
            dst_ref=scales_ref.at[slot],
            send_sem=s_send,
            recv_sem=s_recv,
            device_id=device(lax.rem(z + o // 2, 8), x, y, lax.rem(c + o, 2)),
            device_id_type=MESH,
        ).start()

    scales = scales_ref.at[pl.ds(0, GROUP - 1)]
    pltpu.make_async_copy(scales, scales, s_recv).wait()
    pltpu.make_async_copy(scales, scales, s_send).wait()
    parts = half.at[:, pl.ds(0, GROUP - 1)]
    pltpu.make_async_copy(parts, parts, b_send).wait()
    arrived = out_ref.at[pl.ds(0, GROUP - 1)]
    pltpu.make_async_copy(arrived, arrived, a_send).wait()
    pltpu.make_async_copy(arrived, arrived, a_recv).wait()
    keep.wait()


def order_kernel(order_ref, block_ref, data_ref, scales_ref, out_ref, lines_ref, got, scaled, in_sem, out_sem):
    count = out_ref.shape[0]

    def fetch(p):
        e = order_ref[p]
        return pltpu.make_async_copy(data_ref.at[lax.rem(e, 16), e // 16], got.at[p], in_sem.at[p])

    def store(p):
        return pltpu.make_async_copy(scaled.at[p], out_ref.at[p], out_sem.at[p])

    @pl.loop(0, count)
    def _(p):
        fetch(p).start()

    diagonal = lax.broadcasted_iota(jnp.int32, (COS, HAD), 0) == lax.broadcasted_iota(
        jnp.int32, (COS, HAD), 1
    )
    low = block_ref[0]

    @pl.loop(0, count)
    def _(p):
        e = order_ref[p]
        for b in range(2):
            lines_ref[p, b : b + 1, :] = scales_ref[lax.rem(e, 16), b, pl.ds(e // 16, 1), :][:, :COS]
        line = scales_ref[lax.rem(e, 16), low, pl.ds(e // 16, 1), :]
        column = jnp.sum(jnp.where(diagonal, line, 0.0), axis=1, keepdims=True)
        factor = jnp.broadcast_to(1.0 / column, (COS, HAD))
        fetch(p).wait()
        for k in range(COS):
            cell = got[p, :, k * HAD : (k + 1) * HAD].astype(jnp.float32) * factor[k : k + 1, :]
            scaled[p, :, k * HAD : (k + 1) * HAD] = cell.astype(jnp.bfloat16)
        store(p).start()

    @pl.loop(0, count)
    def _(p):
        store(p).wait()


def per_device(weights, owner_map):
    bf16, f32 = jnp.bfloat16, jnp.float32
    had = np.kron(np.eye(2, dtype=np.float32), hadamard()).astype(ml_dtypes.bfloat16)
    mix = np.kron(cosine(), np.eye(ROWS, dtype=np.float32)).astype(ml_dtypes.bfloat16)
    vmem = pl.BlockSpec(memory_space=pltpu.VMEM)
    anywhere = pl.BlockSpec(memory_space=pl.ANY)
    moved, scales = pl.pallas_call(
        move_kernel,
        out_shape=(
            jax.ShapeDtypeStruct((GROUP, 2, 8, D), bf16),
            jax.ShapeDtypeStruct((GROUP, 2, 8, HAD), f32),
        ),
        in_specs=[anywhere, vmem, vmem],
        out_specs=(anywhere, vmem),
        scratch_shapes=[
            pltpu.VMEM((WAVES, GROUP, ROWS, WIDE), bf16),
            pltpu.VMEM((WAVES, GROUP, ROWS, WIDE), bf16),
            pltpu.VMEM((WAVES, GROUP, ROWS, WIDE), bf16),
            pltpu.VMEM((COS * ROWS, 2 * HAD), f32),
            pltpu.VMEM((WAVES, 2, 2, 8, D), bf16),
            pltpu.VMEM((2, COS, 8, HAD), f32),
            pltpu.VMEM((2, 8, HAD), f32),
            pltpu.SemaphoreType.DMA((WAVES,)),
            pltpu.SemaphoreType.DMA,
            pltpu.SemaphoreType.DMA((WAVES,)),
            pltpu.SemaphoreType.DMA,
            pltpu.SemaphoreType.DMA,
            pltpu.SemaphoreType.DMA,
            pltpu.SemaphoreType.DMA((2,)),
            pltpu.SemaphoreType.DMA,
            pltpu.SemaphoreType.DMA,
        ],
        compiler_params=pltpu.CompilerParams(
            collective_id=0, has_side_effects=True, vmem_limit_bytes=48 * 2**20
        ),
        name="move",
    )(weights.reshape(GROUP, WAVES, ROWS, WIDE), jnp.asarray(had), jnp.asarray(mix))
    count = owner_map.shape[0]
    quant, lines = pl.pallas_call(
        order_kernel,
        out_shape=(
            jax.ShapeDtypeStruct((count, 8, D), bf16),
            jax.ShapeDtypeStruct((count, 2, COS), f32),
        ),
        in_specs=[
            pl.BlockSpec(memory_space=pltpu.SMEM),
            pl.BlockSpec(memory_space=pltpu.SMEM),
            anywhere,
            vmem,
        ],
        out_specs=(anywhere, vmem),
        scratch_shapes=[
            pltpu.VMEM((count, 8, D), bf16),
            pltpu.VMEM((count, 8, D), bf16),
            pltpu.SemaphoreType.DMA((count,)),
            pltpu.SemaphoreType.DMA((count,)),
        ],
        compiler_params=pltpu.CompilerParams(vmem_limit_bytes=32 * 2**20),
        name="order",
    )(positions(owner_map), (lax.axis_index("ep") // 8).reshape(1), moved, scales)
    return quant.reshape(count, 1, 8, D), lines


def solution(mesh):
    return jax.shard_map(
        per_device,
        mesh=mesh,
        in_specs=(P(("ep", "rep"), None, "fsdp"), P()),
        out_specs=(P(None, "fsdp", ("ep", "rep"), None), P(None, "fsdp", None)),
        check_vma=False,
    )
```

time: 300 us -> 119 us (0.40)
  Pallas kernels: 0 us -> 113 us
  blocking collectives: 109 us -> 0 us
  local copies, waits for them, and re-layouts: 86.4 us -> 2.32 us
  waiting for transfers between devices: 43.6 us -> 0 us
  other arithmetic: 30.9 us -> 1.03 us
  starting transfers between devices: 16.5 us -> 0 us
  matrix products: 8.3 us -> 0 us
    pallas_call x0 -> x2, Pallas kernels: none -> 113 us  [the longest x1 101 us: per_device(): pl.pallas_call(move_kernel, out_shape=(jax.ShapeDtypeStruct((GROUP, 2, 8,...]
    all_gather x1 -> x0, blocking collectives: 109 us -> none  [per_device(): all_scales = lax.all_gather(block_scale, ('ep', 'rep'), axis=0, tiled=True)]
    all_to_all x2 -> x0, waiting for transfers between devices: 43.6 us -> none  [the longest x1 43.6 us: per_device(): lax.all_to_all(half_turned, 'fsdp', split_axis=1, concat_axis=4, tiled=True)]
    unnamed x7 -> x4, local copies, waits for them, and re-layouts: 40.8 us -> 2.32 us
    unnamed x3 -> x0, other arithmetic: 27.4 us -> none
    another operation x2 -> x0, local copies, waits for them, and re-layouts: 26.9 us -> none  [the longest x1 19.7 us: per_device(): scaled = scaled.reshape(experts_here, row_count // pieces, D)]
    all_to_all x2 -> x0, starting transfers between devices: 16.5 us -> none  [the longest x1 9.13 us: per_device(): lax.all_to_all(scaled, ('ep', 'rep'), split_axis=1, concat_axis=0, tiled=...]
    reshape x2 -> x0, local copies, waits for them, and re-layouts: 13.4 us -> none  [per_device(): half_flat.reshape(experts_here, pieces, blocks_each, QB, width_here)]
  transfers between devices with their start and end apart: 2 -> 0, of which waited for: 1 -> 0; matrix products, arithmetic and copies ran while one was open for 1% -> 0% of each run, Pallas kernels for 0% -> 0%
where the time goes in v1:
time: 119 us; the launch traced here: 117 us
  Pallas kernels  113 us (95%)
  local copies, waits for them, and re-layouts  2.32 us (2%)
    pallas_call x1, Pallas kernels, per_device(): pl.pallas_call(move_kernel, out_shape=(jax.ShapeDtypeStruct((GROUP, 2, 8,...  101 us
    pallas_call x1, Pallas kernels, per_device(): pl.pallas_call(order_kernel, out_shape=(jax.ShapeDtypeStruct((count, 8, D...  11.7 us

profile of v1, /device:TPU:8, one launch (start us, length us, event | category | flops | bytes accessed | tf_op | source)
XLA Modules:
  0.0 116.9 jit_solution(9802970928010012337)
XLA Ops:
  0.6 0.9 convert_reduce_fusion
  1.6 0.1 select_reduce_fusion.order_ref
  1.7 0.0 copy-start
  1.7 1.4 %copy-done = bf16[896,896]{1,0:T(8,128)(2,1)S(1)} copy-done((bf16[896,896]{1,0:T(8,128)(2,1)S(1)}, bf16[896,896]{1,0:T(8,128)(2,1)}, u32[]{:S(2)}) %copy-start) | copy-done | bytes 1605656
  3.1 0.0 copy-start.1
  3.1 0.9 copy-done.1
  4.0 101.1 %move.1 = (bf16[16,2,8,7168]{3,2,1,0:T(8,128)(2,1)S(1)}, f32[16,2,8,128]{3,2,1,0:T(8,128)S(1)}) custom-call(bf16[16,8,16,896]{3,2,1,0:T(8,128)(2,1)} %bitcast.5, bf16[256,256]{1,0:T(8,128)(2,1)S(1)} %copy-done.1, bf16[896,896]{1,0:T(8,128)(2,1)S(1)} %copy-done), custom_call_target="tpu_custom_call" | custom-call | tf_op jit(solution)/shard_map/move/pallas_call | solution.py:268
  105.1 11.7 %order.1 = (bf16[32,8,7168]{2,1,0:T(8,128)(2,1)}, f32[32,2,56]{2,1,0:T(2,128)}) custom-call(s32[32]{0:T(128)S(1)} %select_reduce_fusion.order_ref, s32[1]{0:T(128)} %bitcast.block_ref, bf16[16,2,8,7168]{3,2,1,0:T(8,128)(2,1)S(1)} %get-tuple-element.6.data_ref, f32[16,2,8,128]{3,2,1,0:T(8,128)S(1)} %get-tuple-element.7.scales_ref), custom_call_target="tpu_custom_call" | custom-call | tf_op jit(solution)/shard_map/order/pallas_call | solution.py:300
Async XLA Ops:
  1.7 1.4 %copy-start = (bf16[896,896]{1,0:T(8,128)(2,1)S(1)}, bf16[896,896]{1,0:T(8,128)(2,1)}, u32[]{:S(2)}) copy-start(bf16[896,896]{1,0:T(8,128)(2,1)} %constant.27.clone.mix_ref) | copy-start | bytes 4816900
  3.1 0.9 copy-start.1

commit v2 on v1

v2 whole, which is shorter than its diff:
```python
import math

import jax
import jax.numpy as jnp
import ml_dtypes
import numpy as np
from jax import lax
from jax.experimental import pallas as pl
from jax.experimental.pallas import tpu as pltpu
from jax.sharding import PartitionSpec as P

MESH = pl.DeviceIdType.MESH
D = 7168
HAD = 128
COS = 56
WIDE = 896
TILES = WIDE // HAD
ROWS = 16
WAVES = 8
HELD = 3
GROUP = 16
EPS = 1e-06


def hadamard():
    i = np.arange(HAD)
    both = i[:, None] & i[None, :]
    ones = sum((both >> bit) & 1 for bit in range(7))
    return (1 - 2 * (ones % 2)).astype(np.float32)


def cosine():
    k = np.arange(COS, dtype=np.float64)[:, None]
    j = np.arange(COS, dtype=np.float64)[None, :]
    c = np.sqrt(2.0 / COS) * np.cos(np.pi * (2 * j + 1) * k / (2 * COS))
    c[0] *= np.sqrt(0.5)
    return c.astype(ml_dtypes.bfloat16).astype(np.float32)


def device(z, x, y, c):
    return (lax.rem(x, 2) * 8 + z, y * 2 + x // 2, c)


def place():
    ep, fsdp, core = lax.axis_index("ep"), lax.axis_index("fsdp"), lax.axis_index("rep")
    return lax.rem(ep, 8), lax.rem(fsdp, 2) * 2 + ep // 8, fsdp // 2, core


def wave_step(i):
    return 4 + (1 - 2 * lax.rem(i, 2)) * ((i + 1) // 2)


def column_of(line, mask):
    return jnp.sum(jnp.where(mask, line, 0.0), axis=1, keepdims=True)


def diagonal(rows, lanes):
    return lax.broadcasted_iota(jnp.int32, (rows, lanes), 0) == lax.broadcasted_iota(
        jnp.int32, (rows, lanes), 1
    )


def move_kernel(
    w_ref, had_hbm, mix_hbm, owner_ref, out_ref, scales_ref, order_ref,
    had_ref, mix_ref, w_buf, half, turned, res, sent, arrived, top, lines, tops, factors,
    t_sem, w_sem, p_sem, b_send, b_recv, a_send, a_recv, pair_sem, s_send, s_recv,
):
    z, x, y, c = place()
    here = y * 4 + x
    slot = z * 2 + c
    low = lax.rem(x, 2)
    across = lax.rem(z + 4, 8)

    barrier = pltpu.get_barrier_semaphore()
    for dz in range(8):
        for dc in range(2):
            if dz or dc:
                pl.semaphore_signal(
                    barrier, inc=1, device_id_type=MESH,
                    device_id=device(lax.rem(z + dz, 8), x, y, lax.rem(c + dc, 2)),
                )
    for o in range(1, GROUP):
        pl.semaphore_signal(
            barrier, inc=1, device_id_type=MESH,
            device_id=device(z, lax.rem(x + o % 4, 4), lax.rem(y + o // 4, 4), c),
        )

    def goes_to(i):
        return lax.rem(z + wave_step(i), 8)

    def fetch(i):
        return pltpu.make_async_copy(w_ref.at[:, goes_to(i)], w_buf.at[i], w_sem.at[i])

    get_had = pltpu.make_async_copy(had_hbm, had_ref, t_sem.at[0])
    get_mix = pltpu.make_async_copy(mix_hbm, mix_ref, t_sem.at[1])
    get_had.start()

    @pl.loop(0, WAVES)
    def _(i):
        fetch(i).start()

    get_mix.start()

    top[...] = jnp.zeros_like(top)

    def turn(i):
        fetch(i).wait()
        rows = w_buf[i].reshape(GROUP * ROWS, WIDE)
        for first in range(0, WIDE, 256):
            wide = min(256, WIDE - first)
            got = jnp.dot(
                rows[:, first : first + wide], had_ref[:wide, :wide], preferred_element_type=jnp.float32
            ) * jnp.float32(1.0 / math.sqrt(HAD))
            half[i, :, :, first : first + wide] = got.astype(jnp.bfloat16).reshape(GROUP, ROWS, wide)

    def spread(source, i):
        turned[i, here] = half[source, here]

        @pl.loop(1, GROUP)
        def _(o):
            to_x, to_y = lax.rem(x + lax.rem(o, 4), 4), lax.rem(y + o // 4, 4)
            pltpu.make_async_remote_copy(
                src_ref=half.at[source, to_y * 4 + to_x],
                dst_ref=turned.at[i, here],
                send_sem=b_send,
                recv_sem=b_recv.at[i],
                device_id=device(z, to_x, to_y, c),
                device_id_type=MESH,
            ).start()

    def send(i, to_z, into, to_c):
        pltpu.make_async_remote_copy(
            src_ref=sent.at[i, to_c],
            dst_ref=arrived.at[into],
            send_sem=a_send,
            recv_sem=a_recv.at[into],
            device_id=device(to_z, x, y, to_c),
            device_id_type=MESH,
        ).start()

    def ship(i, to_c):
        send(i, goes_to(i), slot, to_c)

    get_had.wait()
    turn(0)
    pl.semaphore_wait(barrier, 30)
    over = pltpu.make_async_remote_copy(
        src_ref=half.at[0],
        dst_ref=half.at[WAVES],
        send_sem=p_sem.at[0],
        recv_sem=p_sem.at[1],
        device_id=device(across, x, y, c),
        device_id_type=MESH,
    )
    over.start()
    turn(1)
    spread(1, 1)
    get_mix.wait()

    ids = (lax.broadcasted_iota(jnp.int32, (32, 32), 0), lax.broadcasted_iota(jnp.int32, (32, 32), 1))
    owner = jnp.broadcast_to(owner_ref[...], (32, 32)).astype(jnp.float32)
    other = column_of(owner, diagonal(32, 32))
    before = (owner < other) | ((owner == other) & (ids[1] < ids[0]))
    position = jnp.sum(before.astype(jnp.float32), axis=1, keepdims=True)
    chosen = jnp.where(position == ids[1].astype(jnp.float32), ids[0].astype(jnp.float32), 0.0)
    order_ref[...] = jnp.sum(chosen, axis=0, keepdims=True).astype(jnp.int32)

    @pl.loop(0, WAVES)
    def _(step):
        i = lax.rem(step + 1, WAVES)
        crossed = i == 0

        @pl.when(step < WAVES - 2)
        def _():
            turn(i + 1)
            spread(i + 1, i + 1)

        @pl.when(step == WAVES - 2)
        def _():
            over.wait()
            spread(WAVES, 0)

        landed = turned.at[i, pl.ds(0, GROUP - 1)]
        pltpu.make_async_copy(landed, landed, b_recv.at[i]).wait()

        cells = [
            jnp.concatenate(
                [
                    turned[i, f * 2 + e, :, t * HAD : (t + 1) * HAD]
                    for f in range(8)
                    for t in range(TILES)
                ],
                axis=0,
            )
            for e in range(2)
        ]
        res[...] = jnp.dot(
            mix_ref[...], jnp.concatenate(cells, axis=1), preferred_element_type=jnp.float32
        )
        which = jnp.where(crossed, 1, 0)
        for k in range(COS):
            for e in range(2):
                best = top[which, e, k]
                for to_c in range(2):
                    got = res[k * ROWS + to_c * 8 : k * ROWS + to_c * 8 + 8, e * HAD : (e + 1) * HAD]
                    best = jnp.maximum(best, jnp.abs(got))
                    sent[i, to_c, e, :, k * HAD : (k + 1) * HAD] = got.astype(jnp.bfloat16)
                top[which, e, k] = best

        @pl.when(step < HELD)
        def _():
            ship(i, 0)
            ship(i, 1)

        @pl.when(step >= WAVES - 2)
        def _():
            into = jnp.where(crossed, across * 2 + c, slot)
            send(i, z, into, 1 - c)
            pltpu.make_async_copy(sent.at[i, c], arrived.at[into], a_recv.at[into]).start()

    mask = diagonal(COS, HAD)
    rows = []
    for which in range(2):
        largest = jnp.max(jnp.max(top[which], axis=2), axis=2, keepdims=True)
        rows += [jnp.sum(jnp.where(mask, largest[e], 0.0), axis=0, keepdims=True) for e in range(2)]
    mine = jnp.concatenate(rows + [jnp.zeros((4, HAD), jnp.float32)], axis=0)
    lines[...] = mine
    tops[slot] = mine

    @pl.loop(1, GROUP)
    def _(o):
        pltpu.make_async_remote_copy(
            src_ref=lines,
            dst_ref=tops.at[slot],
            send_sem=s_send,
            recv_sem=s_recv,
            device_id=device(lax.rem(z + o // 2, 8), x, y, lax.rem(c + o, 2)),
            device_id_type=MESH,
        ).start()

    @pl.loop(HELD, WAVES - 2)
    def _(step):
        ship(step + 1, 0)
        ship(step + 1, 1)

    others = tops.at[pl.ds(0, GROUP - 1)]
    pltpu.make_async_copy(others, others, s_recv).wait()
    for e in range(2):
        crossing = jnp.concatenate([tops[8:, 2 + e, :], tops[:8, 2 + e, :]], axis=0)
        scales_ref[low, e] = jnp.maximum(tops[:, e, :], crossing) + jnp.float32(EPS)
    pair = pltpu.make_async_remote_copy(
        src_ref=scales_ref.at[low],
        dst_ref=scales_ref.at[low],
        send_sem=pair_sem.at[0],
        recv_sem=pair_sem.at[1],
        device_id=device(z, x + 1 - 2 * low, y, c),
        device_id_type=MESH,
    )
    pair.start()

    @pl.loop(0, GROUP)
    def _(s):
        for e in range(2):
            column = column_of(scales_ref[low, e, pl.ds(s, 1), :], mask)
            factors[s, e] = jnp.broadcast_to(1.0 / column, (COS, HAD))

    @pl.loop(0, GROUP)
    def _(step):
        from_z = lax.rem(z + 8 - wave_step(lax.rem(step // 2 + 7, 8)), 8)
        s = from_z * 2 + lax.rem(step, 2)
        pltpu.make_async_copy(arrived.at[s], arrived.at[s], a_recv.at[s]).wait()
        for e in range(2):
            for k in range(COS):
                cell = arrived[s, e, :, k * HAD : (k + 1) * HAD].astype(jnp.float32)
                cell = cell * factors[s, e, k : k + 1, :]
                out_ref[s, e, :, k * HAD : (k + 1) * HAD] = cell.astype(jnp.bfloat16)

    pltpu.make_async_copy(others, others, s_send).wait()
    pair.wait()
    parts = half.at[pl.ds(0, WAVES), pl.ds(0, GROUP - 1)]
    pltpu.make_async_copy(parts, parts, b_send).wait()
    shipped = arrived.at[pl.ds(0, GROUP - 2)]
    pltpu.make_async_copy(shipped, shipped, a_send).wait()


def order_kernel(order_ref, data_ref, scales_ref, out_ref, lines_ref, lines, sem, lines_sem):
    count = out_ref.shape[0]

    @pl.loop(0, count)
    def _(p):
        e = order_ref[0, p]
        pltpu.make_async_copy(data_ref.at[lax.rem(e, GROUP), e // GROUP], out_ref.at[p], sem).start()

    @pl.loop(0, count)
    def _(p):
        e = order_ref[0, p]
        for b in range(2):
            lines[p, b : b + 1, :] = scales_ref[b, e // GROUP, pl.ds(lax.rem(e, GROUP), 1), :][:, :COS]

    put = pltpu.make_async_copy(lines, lines_ref, lines_sem)
    put.start()
    pltpu.make_async_copy(out_ref, out_ref, sem).wait()
    put.wait()


def per_device(weights, owner_map):
    bf16, f32 = jnp.bfloat16, jnp.float32
    had = np.kron(np.eye(2, dtype=np.float32), hadamard()).astype(ml_dtypes.bfloat16)
    mix = np.kron(cosine(), np.eye(ROWS, dtype=np.float32)).astype(ml_dtypes.bfloat16)
    vmem = pl.BlockSpec(memory_space=pltpu.VMEM)
    smem = pl.BlockSpec(memory_space=pltpu.SMEM)
    anywhere = pl.BlockSpec(memory_space=pl.ANY)
    hbm = pl.BlockSpec(memory_space=pltpu.HBM)
    count = owner_map.shape[0]
    dma = pltpu.SemaphoreType.DMA
    moved, scales, order = pl.pallas_call(
        move_kernel,
        out_shape=(
            pltpu.VMEM((GROUP, 2, 8, D), bf16),
            pltpu.VMEM((2, 2, GROUP, HAD), f32),
            jax.ShapeDtypeStruct((1, count), jnp.int32),
        ),
        in_specs=[hbm, hbm, hbm, vmem],
        out_specs=(vmem, vmem, vmem),
        scratch_shapes=[
            pltpu.VMEM(had.shape, bf16),
            pltpu.VMEM(mix.shape, bf16),
            pltpu.VMEM((WAVES, GROUP, ROWS, WIDE), bf16),
            pltpu.VMEM((WAVES + 1, GROUP, ROWS, WIDE), bf16),
            pltpu.VMEM((WAVES, GROUP, ROWS, WIDE), bf16),
            pltpu.VMEM((COS * ROWS, 2 * HAD), f32),
            pltpu.VMEM((WAVES, 2, 2, 8, D), bf16),
            pltpu.VMEM((GROUP, 2, 8, D), bf16),
            pltpu.VMEM((2, 2, COS, 8, HAD), f32),
            pltpu.VMEM((8, HAD), f32),
            pltpu.VMEM((GROUP, 8, HAD), f32),
            pltpu.VMEM((GROUP, 2, COS, HAD), f32),
            dma((2,)),
            dma((WAVES,)),
            dma((2,)),
            dma,
            dma((WAVES,)),
            dma,
            dma((GROUP,)),
            dma((2,)),
            dma,
            dma,
        ],
        compiler_params=pltpu.CompilerParams(
            collective_id=0, has_side_effects=True, vmem_limit_bytes=52 * 2**20
        ),
        name="move",
    )(
        weights.reshape(GROUP, WAVES, ROWS, WIDE),
        jnp.asarray(had),
        jnp.asarray(mix),
        owner_map.reshape(1, count),
    )
    quant, lines = pl.pallas_call(
        order_kernel,
        out_shape=(
            jax.ShapeDtypeStruct((count, 8, D), bf16),
            jax.ShapeDtypeStruct((count, 2, COS), f32),
        ),
        in_specs=[smem, vmem, vmem],
        out_specs=(anywhere, anywhere),
        scratch_shapes=[pltpu.VMEM((count, 2, COS), f32), dma, dma],
        compiler_params=pltpu.CompilerParams(vmem_limit_bytes=8 * 2**20),
        name="order",
    )(order, moved, scales)
    return quant.reshape(count, 1, 8, D), lines


def solution(mesh):
    return jax.shard_map(
        per_device,
        mesh=mesh,
        in_specs=(P(("ep", "rep"), None, "fsdp"), P()),
        out_specs=(P(None, "fsdp", ("ep", "rep"), None), P(None, "fsdp", None)),
        check_vma=False,
    )
```

time: 119 us -> 99.1 us (0.83)
  the two profiles are of different devices: /device:TPU:8 before, /device:TPU:1 now
where the time goes in v2:
time: 99.1 us; the launch traced here: 99 us
  Pallas kernels  97.7 us (99%)
    pallas_call x1, Pallas kernels, per_device(): pl.pallas_call(move_kernel, out_shape=(pltpu.VMEM((GROUP, 2, 8, D), bf16)...  95.3 us
    pallas_call x1, Pallas kernels, per_device(): pl.pallas_call(order_kernel, out_shape=(jax.ShapeDtypeStruct((count, 8, D...  2.38 us

profile of v2, /device:TPU:1, one launch (start us, length us, event | category | flops | bytes accessed | tf_op | source)
XLA Modules:
  0.0 99.0 jit_solution(5294323436898930606)
XLA Ops:
  0.6 95.3 %move.1 = (bf16[16,2,8,7168]{3,2,1,0:T(8,128)(2,1)S(1)}, f32[2,2,16,128]{3,2,1,0:T(8,128)S(1)}, s32[1,32]{1,0:T(1,128)}) custom-call(bf16[16,8,16,896]{3,2,1,0:T(8,128)(2,1)} %bitcast.5, bf16[256,256]{1,0:T(8,128)(2,1)} %constant.4.clone.had_hbm, bf16[896,896]{1,0:T(8,128)(2,1)} %constant.5.clone.mix_hbm, s32[1,32]{1,0:T(1,128)} %bitcast.6), custom_call_target="tpu_custom_call" | custom-call | tf_op jit(solution)/shard_map/move/pallas_call | solution.py:316
  96.0 0.0 copy-start
  96.0 0.7 copy-done
  96.6 2.4 %order.1 = (bf16[32,8,7168]{2,1,0:T(8,128)(2,1)}, f32[32,2,56]{2,1,0:T(2,128)}) custom-call(s32[1,32]{1,0:T(1,128)S(1)} %copy-done, bf16[16,2,8,7168]{3,2,1,0:T(8,128)(2,1)S(1)} %get-tuple-element.8.data_ref, f32[2,2,16,128]{3,2,1,0:T(8,128)S(1)} %get-tuple-element.9.scales_ref), custom_call_target="tpu_custom_call" | custom-call | tf_op jit(solution)/shard_map/order/pallas_call | solution.py:359
Async XLA Ops:
  96.0 0.7 copy-start

commit v3 on v2

--- a/solution.py
+++ b/solution.py
@@ -17,7 +17,8 @@
 TILES = WIDE // HAD
 ROWS = 16
 WAVES = 8
-HELD = 3
+HELD = 2
+LAST = 4
 GROUP = 16
 EPS = 1e-06
 
@@ -71,8 +72,19 @@
     low = lax.rem(x, 2)
     across = lax.rem(z + 4, 8)
 
+    def goes_to(i):
+        return lax.rem(z + wave_step(i), 8)
+
+    def fetch(i):
+        return pltpu.make_async_copy(w_ref.at[:, goes_to(i)], w_buf.at[i], w_sem.at[i])
+
+    get_had = pltpu.make_async_copy(had_hbm, had_ref, t_sem.at[0])
+    get_mix = pltpu.make_async_copy(mix_hbm, mix_ref, t_sem.at[1])
+    get_had.start()
+    fetch(0).start()
+
     barrier = pltpu.get_barrier_semaphore()
-    for dz in range(8):
+    for dz in (4, 3, 5, 2, 6, 1, 7, 0):
         for dc in range(2):
             if dz or dc:
                 pl.semaphore_signal(
@@ -85,23 +97,11 @@
             device_id=device(z, lax.rem(x + o % 4, 4), lax.rem(y + o // 4, 4), c),
         )
 
-    def goes_to(i):
-        return lax.rem(z + wave_step(i), 8)
-
-    def fetch(i):
-        return pltpu.make_async_copy(w_ref.at[:, goes_to(i)], w_buf.at[i], w_sem.at[i])
-
-    get_had = pltpu.make_async_copy(had_hbm, had_ref, t_sem.at[0])
-    get_mix = pltpu.make_async_copy(mix_hbm, mix_ref, t_sem.at[1])
-    get_had.start()
-
-    @pl.loop(0, WAVES)
+    @pl.loop(1, WAVES)
     def _(i):
         fetch(i).start()
 
     get_mix.start()
-
-    top[...] = jnp.zeros_like(top)
 
     def turn(i):
         fetch(i).wait()
@@ -155,6 +155,7 @@
     over.start()
     turn(1)
     spread(1, 1)
+    top[...] = jnp.zeros_like(top)
     get_mix.wait()
 
     ids = (lax.broadcasted_iota(jnp.int32, (32, 32), 0), lax.broadcasted_iota(jnp.int32, (32, 32), 1))
@@ -238,7 +239,7 @@
             device_id_type=MESH,
         ).start()
 
-    @pl.loop(HELD, WAVES - 2)
+    @pl.loop(HELD, LAST)
     def _(step):
         ship(step + 1, 0)
         ship(step + 1, 1)
@@ -258,6 +259,11 @@
     )
     pair.start()
 
+    @pl.loop(LAST, WAVES - 2)
+    def _(step):
+        ship(step + 1, 0)
+        ship(step + 1, 1)
+
     @pl.loop(0, GROUP)
     def _(s):
         for e in range(2):
@@ -283,8 +289,13 @@
     pltpu.make_async_copy(shipped, shipped, a_send).wait()
 
 
-def order_kernel(order_ref, data_ref, scales_ref, out_ref, lines_ref, lines, sem, lines_sem):
+def order_kernel(
+    order_vmem, data_ref, scales_ref, out_ref, lines_ref, order_ref, lines, sem, lines_sem, order_sem
+):
     count = out_ref.shape[0]
+    get_order = pltpu.make_async_copy(order_vmem, order_ref, order_sem)
+    get_order.start()
+    get_order.wait()
 
     @pl.loop(0, count)
     def _(p):
@@ -308,7 +319,6 @@
     had = np.kron(np.eye(2, dtype=np.float32), hadamard()).astype(ml_dtypes.bfloat16)
     mix = np.kron(cosine(), np.eye(ROWS, dtype=np.float32)).astype(ml_dtypes.bfloat16)
     vmem = pl.BlockSpec(memory_space=pltpu.VMEM)
-    smem = pl.BlockSpec(memory_space=pltpu.SMEM)
     anywhere = pl.BlockSpec(memory_space=pl.ANY)
     hbm = pl.BlockSpec(memory_space=pltpu.HBM)
     count = owner_map.shape[0]
@@ -318,7 +328,7 @@
         out_shape=(
             pltpu.VMEM((GROUP, 2, 8, D), bf16),
             pltpu.VMEM((2, 2, GROUP, HAD), f32),
-            jax.ShapeDtypeStruct((1, count), jnp.int32),
+            pltpu.VMEM((1, count), jnp.int32),
         ),
         in_specs=[hbm, hbm, hbm, vmem],
         out_specs=(vmem, vmem, vmem),
@@ -362,9 +372,15 @@
             jax.ShapeDtypeStruct((count, 8, D), bf16),
             jax.ShapeDtypeStruct((count, 2, COS), f32),
         ),
-        in_specs=[smem, vmem, vmem],
+        in_specs=[vmem, vmem, vmem],
         out_specs=(anywhere, anywhere),
-        scratch_shapes=[pltpu.VMEM((count, 2, COS), f32), dma, dma],
+        scratch_shapes=[
+            pltpu.SMEM((1, count), jnp.int32),
+            pltpu.VMEM((count, 2, COS), f32),
+            dma,
+            dma,
+            dma,
+        ],
         compiler_params=pltpu.CompilerParams(vmem_limit_bytes=8 * 2**20),
         name="order",
     )(order, moved, scales)

time: 99.1 us -> 97.9 us (0.988)
  no operation moved by 1% of the time
where the time goes in v3:
time: 97.9 us; the launch traced here: 97.8 us
  Pallas kernels  97.2 us (99%)
    pallas_call x1, Pallas kernels, per_device(): pl.pallas_call(move_kernel, out_shape=(pltpu.VMEM((GROUP, 2, 8, D), bf16)...  94.8 us
    pallas_call x1, Pallas kernels, per_device(): pl.pallas_call(order_kernel, out_shape=(jax.ShapeDtypeStruct((count, 8, D...  2.39 us

profile of v3, /device:TPU:1, one launch (start us, length us, event | category | flops | bytes accessed | tf_op | source)
XLA Modules:
  0.0 97.8 jit_solution(5248914185472647642)
XLA Ops:
  0.6 94.8 %move.1 = (bf16[16,2,8,7168]{3,2,1,0:T(8,128)(2,1)S(1)}, f32[2,2,16,128]{3,2,1,0:T(8,128)S(1)}, s32[1,32]{1,0:T(1,128)S(1)}) custom-call(bf16[16,8,16,896]{3,2,1,0:T(8,128)(2,1)} %bitcast.5, bf16[256,256]{1,0:T(8,128)(2,1)} %constant.4.clone.had_hbm, bf16[896,896]{1,0:T(8,128)(2,1)} %constant.5.clone.mix_hbm, s32[1,32]{1,0:T(1,128)} %bitcast.6), custom_call_target="tpu_custom_call" | custom-call | tf_op jit(solution)/shard_map/move/pallas_call | solution.py:326
  95.4 2.4 %order.1 = (bf16[32,8,7168]{2,1,0:T(8,128)(2,1)}, f32[32,2,56]{2,1,0:T(2,128)}) custom-call(s32[1,32]{1,0:T(1,128)S(1)} %get-tuple-element.7.order_vmem, bf16[16,2,8,7168]{3,2,1,0:T(8,128)(2,1)S(1)} %get-tuple-element.8.data_ref, f32[2,2,16,128]{3,2,1,0:T(8,128)S(1)} %get-tuple-element.9.scales_ref), custom_call_target="tpu_custom_call" | custom-call | tf_op jit(solution)/shard_map/order/pallas_call | solution.py:369

commit v4 on v3

--- a/solution.py
+++ b/solution.py
@@ -210,8 +210,8 @@
 
         @pl.when(step < HELD)
         def _():
+            ship(i, 1)
             ship(i, 0)
-            ship(i, 1)
 
         @pl.when(step >= WAVES - 2)
         def _():
@@ -241,8 +241,8 @@
 
     @pl.loop(HELD, LAST)
     def _(step):
+        ship(step + 1, 1)
         ship(step + 1, 0)
-        ship(step + 1, 1)
 
     others = tops.at[pl.ds(0, GROUP - 1)]
     pltpu.make_async_copy(others, others, s_recv).wait()
@@ -261,8 +261,8 @@
 
     @pl.loop(LAST, WAVES - 2)
     def _(step):
+        ship(step + 1, 1)
         ship(step + 1, 0)
-        ship(step + 1, 1)
 
     @pl.loop(0, GROUP)
     def _(s):

time: 97.9 us -> 96.2 us (0.983)
  the two profiles are of different devices: /device:TPU:1 before, /device:TPU:8 now
where the time goes in v4:
time: 96.2 us; the launch traced here: 96.1 us
  Pallas kernels  95.5 us (99%)
    pallas_call x1, Pallas kernels, per_device(): pl.pallas_call(move_kernel, out_shape=(pltpu.VMEM((GROUP, 2, 8, D), bf16)...  93.1 us
    pallas_call x1, Pallas kernels, per_device(): pl.pallas_call(order_kernel, out_shape=(jax.ShapeDtypeStruct((count, 8, D...  2.39 us

profile of v4, /device:TPU:8, one launch (start us, length us, event | category | flops | bytes accessed | tf_op | source)
XLA Modules:
  0.0 96.1 jit_solution(3923618548332456774)
XLA Ops:
  0.6 93.1 %move.1 = (bf16[16,2,8,7168]{3,2,1,0:T(8,128)(2,1)S(1)}, f32[2,2,16,128]{3,2,1,0:T(8,128)S(1)}, s32[1,32]{1,0:T(1,128)S(1)}) custom-call(bf16[16,8,16,896]{3,2,1,0:T(8,128)(2,1)} %bitcast.5, bf16[256,256]{1,0:T(8,128)(2,1)} %constant.4.clone.had_hbm, bf16[896,896]{1,0:T(8,128)(2,1)} %constant.5.clone.mix_hbm, s32[1,32]{1,0:T(1,128)} %bitcast.6), custom_call_target="tpu_custom_call" | custom-call | tf_op jit(solution)/shard_map/move/pallas_call | solution.py:326
  93.7 2.4 %order.1 = (bf16[32,8,7168]{2,1,0:T(8,128)(2,1)}, f32[32,2,56]{2,1,0:T(2,128)}) custom-call(s32[1,32]{1,0:T(1,128)S(1)} %get-tuple-element.7.order_vmem, bf16[16,2,8,7168]{3,2,1,0:T(8,128)(2,1)S(1)} %get-tuple-element.8.data_ref, f32[2,2,16,128]{3,2,1,0:T(8,128)S(1)} %get-tuple-element.9.scales_ref), custom_call_target="tpu_custom_call" | custom-call | tf_op jit(solution)/shard_map/order/pallas_call | solution.py:369

commit v5 on v4

--- a/solution.py
+++ b/solution.py
@@ -63,7 +63,7 @@
 
 def move_kernel(
     w_ref, had_hbm, mix_hbm, owner_ref, out_ref, scales_ref, order_ref,
-    had_ref, mix_ref, w_buf, half, turned, res, sent, arrived, top, lines, tops, factors,
+    had_ref, mix_ref, w_buf, half, turned, res, sent, arrived, top, lines, tops, factors, order_vmem,
     t_sem, w_sem, p_sem, b_send, b_recv, a_send, a_recv, pair_sem, s_send, s_recv,
 ):
     z, x, y, c = place()
@@ -164,7 +164,10 @@
     before = (owner < other) | ((owner == other) & (ids[1] < ids[0]))
     position = jnp.sum(before.astype(jnp.float32), axis=1, keepdims=True)
     chosen = jnp.where(position == ids[1].astype(jnp.float32), ids[0].astype(jnp.float32), 0.0)
-    order_ref[...] = jnp.sum(chosen, axis=0, keepdims=True).astype(jnp.int32)
+    order_vmem[...] = jnp.sum(chosen, axis=0, keepdims=True).astype(jnp.int32)
+    put_order = pltpu.make_async_copy(order_vmem, order_ref, t_sem.at[0])
+    put_order.start()
+    put_order.wait()
 
     @pl.loop(0, WAVES)
     def _(step):
@@ -289,13 +292,8 @@
     pltpu.make_async_copy(shipped, shipped, a_send).wait()
 
 
-def order_kernel(
-    order_vmem, data_ref, scales_ref, out_ref, lines_ref, order_ref, lines, sem, lines_sem, order_sem
-):
+def order_kernel(order_ref, data_ref, scales_ref, out_ref, lines_ref, lines, sem, lines_sem):
     count = out_ref.shape[0]
-    get_order = pltpu.make_async_copy(order_vmem, order_ref, order_sem)
-    get_order.start()
-    get_order.wait()
 
     @pl.loop(0, count)
     def _(p):
@@ -319,6 +317,7 @@
     had = np.kron(np.eye(2, dtype=np.float32), hadamard()).astype(ml_dtypes.bfloat16)
     mix = np.kron(cosine(), np.eye(ROWS, dtype=np.float32)).astype(ml_dtypes.bfloat16)
     vmem = pl.BlockSpec(memory_space=pltpu.VMEM)
+    smem = pl.BlockSpec(memory_space=pltpu.SMEM)
     anywhere = pl.BlockSpec(memory_space=pl.ANY)
     hbm = pl.BlockSpec(memory_space=pltpu.HBM)
     count = owner_map.shape[0]
@@ -328,10 +327,10 @@
         out_shape=(
             pltpu.VMEM((GROUP, 2, 8, D), bf16),
             pltpu.VMEM((2, 2, GROUP, HAD), f32),
-            pltpu.VMEM((1, count), jnp.int32),
+            pltpu.SMEM((1, count), jnp.int32),
         ),
         in_specs=[hbm, hbm, hbm, vmem],
-        out_specs=(vmem, vmem, vmem),
+        out_specs=(vmem, vmem, smem),
         scratch_shapes=[
             pltpu.VMEM(had.shape, bf16),
             pltpu.VMEM(mix.shape, bf16),
@@ -345,6 +344,7 @@
             pltpu.VMEM((8, HAD), f32),
             pltpu.VMEM((GROUP, 8, HAD), f32),
             pltpu.VMEM((GROUP, 2, COS, HAD), f32),
+            pltpu.VMEM((1, count), jnp.int32),
             dma((2,)),
             dma((WAVES,)),
             dma((2,)),
@@ -372,12 +372,10 @@
             jax.ShapeDtypeStruct((count, 8, D), bf16),
             jax.ShapeDtypeStruct((count, 2, COS), f32),
         ),
-        in_specs=[vmem, vmem, vmem],
+        in_specs=[smem, vmem, vmem],
         out_specs=(anywhere, anywhere),
         scratch_shapes=[
-            pltpu.SMEM((1, count), jnp.int32),
             pltpu.VMEM((count, 2, COS), f32),
-            dma,
             dma,
             dma,
         ],

time: 96.2 us -> 95.6 us (level)
  no operation moved by 1% of the time
where the time goes in v5:
time: 95.6 us; the launch traced here: 95.5 us
  Pallas kernels  94.9 us (99%)
    pallas_call x1, Pallas kernels, per_device(): pl.pallas_call(move_kernel, out_shape=(pltpu.VMEM((GROUP, 2, 8, D), bf16)...  93.1 us

profile of v5, /device:TPU:8, one launch (start us, length us, event | category | flops | bytes accessed | tf_op | source)
XLA Modules:
  0.0 95.5 jit_solution(17686256361156448452)
XLA Ops:
  0.6 93.1 %move.1 = (bf16[16,2,8,7168]{3,2,1,0:T(8,128)(2,1)S(1)}, f32[2,2,16,128]{3,2,1,0:T(8,128)S(1)}, s32[1,32]{1,0:T(1,128)S(4)}) custom-call(bf16[16,8,16,896]{3,2,1,0:T(8,128)(2,1)} %bitcast.5, bf16[256,256]{1,0:T(8,128)(2,1)} %constant.4.clone.had_hbm, bf16[896,896]{1,0:T(8,128)(2,1)} %constant.5.clone.mix_hbm, s32[1,32]{1,0:T(1,128)} %bitcast.6), custom_call_target="tpu_custom_call" | custom-call | tf_op jit(solution)/shard_map/move/pallas_call | solution.py:325
  93.7 1.8 %order.1 = (bf16[32,8,7168]{2,1,0:T(8,128)(2,1)}, f32[32,2,56]{2,1,0:T(2,128)}) custom-call(s32[1,32]{1,0:T(1,128)S(4)} %get-tuple-element.7.order_ref, bf16[16,2,8,7168]{3,2,1,0:T(8,128)(2,1)S(1)} %get-tuple-element.8.data_ref, f32[2,2,16,128]{3,2,1,0:T(8,128)S(1)} %get-tuple-element.9.scales_ref), custom_call_target="tpu_custom_call" | custom-call | tf_op jit(solution)/shard_map/order/pallas_call | solution.py:369

commit v6 on v5

--- a/solution.py
+++ b/solution.py
@@ -97,12 +97,6 @@
             device_id=device(z, lax.rem(x + o % 4, 4), lax.rem(y + o // 4, 4), c),
         )
 
-    @pl.loop(1, WAVES)
-    def _(i):
-        fetch(i).start()
-
-    get_mix.start()
-
     def turn(i):
         fetch(i).wait()
         rows = w_buf[i].reshape(GROUP * ROWS, WIDE)
@@ -153,6 +147,12 @@
         device_id_type=MESH,
     )
     over.start()
+
+    @pl.loop(1, WAVES)
+    def _(i):
+        fetch(i).start()
+
+    get_mix.start()
     turn(1)
     spread(1, 1)
     top[...] = jnp.zeros_like(top)

time: 95.6 us -> 95.7 us (level)
  no operation moved by 1% of the time
where the time goes in v6:
time: 95.7 us; the launch traced here: 95.5 us
  Pallas kernels  94.9 us (99%)
    pallas_call x1, Pallas kernels, per_device(): pl.pallas_call(move_kernel, out_shape=(pltpu.VMEM((GROUP, 2, 8, D), bf16)...  93.1 us

profile of v6, /device:TPU:8, one launch (start us, length us, event | category | flops | bytes accessed | tf_op | source)
XLA Modules:
  0.0 95.5 jit_solution(299640652459361630)
XLA Ops:
  0.6 93.1 %move.1 = (bf16[16,2,8,7168]{3,2,1,0:T(8,128)(2,1)S(1)}, f32[2,2,16,128]{3,2,1,0:T(8,128)S(1)}, s32[1,32]{1,0:T(1,128)S(4)}) custom-call(bf16[16,8,16,896]{3,2,1,0:T(8,128)(2,1)} %bitcast.5, bf16[256,256]{1,0:T(8,128)(2,1)} %constant.4.clone.had_hbm, bf16[896,896]{1,0:T(8,128)(2,1)} %constant.5.clone.mix_hbm, s32[1,32]{1,0:T(1,128)} %bitcast.6), custom_call_target="tpu_custom_call" | custom-call | tf_op jit(solution)/shard_map/move/pallas_call | solution.py:325
  93.7 1.8 %order.1 = (bf16[32,8,7168]{2,1,0:T(8,128)(2,1)}, f32[32,2,56]{2,1,0:T(2,128)}) custom-call(s32[1,32]{1,0:T(1,128)S(4)} %get-tuple-element.7.order_ref, bf16[16,2,8,7168]{3,2,1,0:T(8,128)(2,1)S(1)} %get-tuple-element.8.data_ref, f32[2,2,16,128]{3,2,1,0:T(8,128)S(1)} %get-tuple-element.9.scales_ref), custom_call_target="tpu_custom_call" | custom-call | tf_op jit(solution)/shard_map/order/pallas_call | solution.py:369
